TPU v7x, 256 devices: a whole 4x4x8 slice. The times are simulated.
256 devices in a mesh: gx: 8 (over x, core), gy: 32 (over z, y).
Axes of the slice: x: 4, y: 4, z: 8, core: 2. Of those that a mesh axis runs over, the one named last changes fastest.
Arguments:
- state_field: float32 [256, 512, 16, 256], P('gx', 'gy'), may hold values from -80 to 80
- start_basis: float32 [256, 32], replicated, may hold values from -6 to 6
Outputs:
- core_tensor: float32 [256, 512, 512], P('gx', 'gy')
- z_factor: float32 [256, 32], replicated
- x_triangle: float32 [256, 256], replicated
All inputs are finite; a program needn't handle non-finite values.
Results may differ from a plain program's by a relative error of at most 0.0003.
Values sent between devices are 32-bit elements; how exact they have to be, the bound alone decides.
A program may use at most 64 MiB of HBM per device.

v0:
```python
import jax
import jax.numpy as jnp
from jax import lax
from jax.sharding import PartitionSpec as P

ITERS = 3


precise = lax.Precision.HIGHEST


def orthonormal(image):
    for repeat in range(2):
        inner_gram = jnp.dot(image.T, image, precision=precise, preferred_element_type=jnp.float32)
        lower_factor = jnp.linalg.cholesky(inner_gram)
        image = lax.linalg.triangular_solve(
            lower_factor, image, left_side=False, lower=True, transpose_a=True
        )
    return image


def local(state_field, start_basis):
    x_cells, y_cells, species, z_cells = state_field.shape
    unfolded = state_field.reshape(x_cells * y_cells * species, z_cells)
    local_gram = lax.dot_general(
        unfolded,
        unfolded,
        (((0,), (0,)), ((), ())),
        precision=precise,
        preferred_element_type=jnp.float32,
    )
    z_basis = start_basis
    gram_z = lax.psum(local_gram, ("gx", "gy"))
    for iteration in range(ITERS):
        z_basis = orthonormal(
            jnp.dot(gram_z, z_basis, precision=precise, preferred_element_type=jnp.float32)
        )
    rank_kept = z_basis.shape[1]
    core_rows = jnp.dot(unfolded, z_basis, precision=precise, preferred_element_type=jnp.float32)
    core_tensor = core_rows.reshape(x_cells, y_cells, species * rank_kept)
    x_total = x_cells * lax.axis_size("gx")
    regrouped = lax.all_to_all(core_tensor, "gx", split_axis=2, concat_axis=0, tiled=True)
    x_rows = regrouped.reshape(x_total, -1)
    local_xgram = jnp.dot(x_rows, x_rows.T, precision=precise, preferred_element_type=jnp.float32)
    gram_x = lax.psum(local_xgram, ("gx", "gy"))
    column_count = y_cells * lax.axis_size("gy") * species * rank_kept
    x_triangle = jnp.linalg.cholesky(gram_x).T / jnp.sqrt(jnp.float32(column_count))
    return (core_tensor, z_basis, x_triangle)


def solution(mesh):
    return jax.shard_map(
        local,
        mesh=mesh,
        in_specs=(P("gx", "gy", None, None), P()),
        out_specs=(P("gx", "gy", None), P(), P()),
        check_vma=False,
    )
```

profile of v0, /device:TPU:1, one launch (start us, length us, event | category | flops | bytes accessed | tf_op | source)
XLA Modules:
  0.0 674.7 jit_solution(2987790697292606197)
XLA Ops:
  7.2 17.8 %convolution_bitcast_fusion.1 = f32[256,256]{1,0:T(8,128)} fusion(f32[32,16,16,256]{3,2,1,0:T(8,128)} %param.5), kind=kOutput, calls=%fused_computation.1 | convolution fusion | flops 6442450944 | bytes 8650752 | tf_op jit(solution)/shard_map/dot_general | solution.py:25
  25.3 252.6 %all-reduce.4.cloned.1.call-done = f32[256,256]{1,0:T(8,128)} async-done(((f32[256,256]{1,0:T(8,128)}), f32[256,256]{1,0:T(8,128)}) %all-reduce.4.cloned.1.call-update) | async-done | bytes 262160 | tf_op jit(solution)/shard_map/psum | solution.py:33
  277.9 1.3 fusion.32
  279.4 2.9 cholesky.222
  283.7 2.4 custom-call.22
  286.6 2.9 cholesky.233
  290.9 2.4 custom-call.23
  293.6 1.3 fusion.35
  295.1 2.9 cholesky.244
  299.4 2.4 custom-call.24
  302.3 2.9 cholesky.255
  306.5 2.4 custom-call.25
  309.2 1.3 fusion.38
  310.8 2.9 cholesky.266
  315.0 2.4 custom-call.26
  318.0 2.9 cholesky.277
  322.2 2.4 custom-call.27
  324.9 9.9 %convolution_bitcast_fusion = f32[8192,32]{0,1:T(8,128)S(1)} fusion(f32[256,32]{0,1:T(8,128)S(1)} %convolution_bitcast_fusion.2, f32[8192,256]{1,0:T(8,128)} %bitcast.127), kind=kOutput, calls=%fused_computation | convolution fusion | flops 805306368 | bytes 9469952 | tf_op jit(solution)/shard_map/dot_general | solution.py:39
  334.8 2.6 copy.47
  337.4 3.5 reshape.41
  341.0 3.8 copy.48
  344.9 3.9 reshape.66
  348.8 21.2 %all_to_all.15 = f32[8,1,32768]{2,1,0:T(1,128)S(1)} all-to-all(f32[8,1,32768]{2,1,0:T(1,128)S(1)} %reshape.66), channel_id=1, replica_groups=mesh['gx'=8,'gy'=32] {'gx'}, dimensions={0} | all-to-all | bytes 2097152 | tf_op jit(solution)/shard_map/all_to_all | solution.py:42
  370.5 3.1 reduce.16
  373.6 3.3 reshape.67
  376.9 3.6 copy.49
  381.1 1.7 fusion.41
  382.9 246.2 %all-reduce.6.cloned.1.call-done = f32[256,256]{0,1:T(8,128)} async-done(((f32[256,256]{0,1:T(8,128)}), f32[256,256]{0,1:T(8,128)}) %all-reduce.6.cloned.1.call-update) | async-done | bytes 262160 | tf_op jit(solution)/shard_map/psum | solution.py:45
  629.0 1.1 copy.51
  631.1 11.7 %cholesky.77 = f32[128,128]{1,0:T(8,128)S(1)} custom-call(f32[128,128]{1,0:T(8,128)S(1)} %cholesky.286), custom_call_target="Cholesky" | custom-call | tf_op jit(solution)/shard_map/jit(cholesky)/cholesky | solution.py:47
  642.9 9.8 %custom-call.16 = f32[1,128,128]{1,2,0:T(8,128)S(1)} custom-call(f32[1,128,128]{2,1,0:T(8,128)S(1)} %get-tuple-element.20), custom_call_target="InvertDiagBlocksLowerTriangular" | custom-call | tf_op jit(solution)/shard_map/jit(cholesky)/cholesky | solution.py:47
  653.2 11.7 %cholesky.132 = f32[128,128]{1,0:T(8,128)S(1)} custom-call(f32[128,128]{1,0:T(8,128)S(1)} %convolution_subtract_fusion), custom_call_target="Cholesky" | custom-call | tf_op jit(solution)/shard_map/jit(cholesky)/cholesky | solution.py:47
  (64 shorter events, 15.4 us)
Async XLA Ops:
  7.2 270.7 %copy-start = (f32[256,32]{0,1:T(8,128)S(1)}, f32[256,32]{0,1:T(8,128)}, u32[]{:S(2)}) copy-start(f32[256,32]{0,1:T(8,128)} %param.6) | copy-start | bytes 98308
  7.2 270.7 %all-reduce.4.cloned.1.call-start = ((), (), s32[]{:S(2)}) async-start(), calls=%async_computation.1 | async-start | bytes 524288 | tf_op jit(solution)/shard_map/psum | solution.py:33
  25.0 604.0 %all-reduce.6.cloned.1.call-start = ((), (), s32[]{:S(2)}) async-start(), calls=%async_computation.2 | async-start | bytes 524288 | tf_op jit(solution)/shard_map/psum | solution.py:45
  324.9 16.1 %copy-start.2 = (f32[256,32]{0,1:T(8,128)}, f32[256,32]{0,1:T(8,128)S(1)}, u32[]{:S(2)}) copy-start(f32[256,32]{0,1:T(8,128)S(1)} %convolution_bitcast_fusion.2) | copy-start | bytes 98308
  341.0 35.9 %copy-start.1 = (f32[32,16,512]{2,1,0:T(8,128)}, f32[32,16,512]{2,1,0:T(8,128)S(1)}, u32[]{:S(2)}) copy-start(f32[32,16,512]{2,1,0:T(8,128)S(1)} %reshape.41) | copy-start | bytes 3145732
Sparse Core Ops, SparseCore 0:
  25.2 252.6 all-reduce.3
  383.0 245.9 all-reduce.5
where the time goes:
time: 676 us; the launch traced here: 675 us
  waiting for transfers between devices  499 us (74%)
  other arithmetic  78.3 us (12%)
  matrix products  36.2 us (5%)
  local copies, waits for them, and re-layouts  24.3 us (4%)
  blocking collectives  21.2 us (3%)
  between operations  15.7 us (2%)
    psum x1, waiting for transfers between devices, local(): gram_z = lax.psum(local_gram, ('gx', 'gy'))  253 us
    psum x1, waiting for transfers between devices, local(): gram_x = lax.psum(local_xgram, ('gx', 'gy'))  246 us
    another operation x6, other arithmetic, local(): jnp.linalg.cholesky(gram_x).T / jnp.sqrt(jnp.float32(column_count))  34 us
    another operation x18, other arithmetic, orthonormal(): lower_factor = jnp.linalg.cholesky(inner_gram)  21.6 us
    all_to_all x1, blocking collectives, local(): lax.all_to_all(core_tensor, 'gx', split_axis=2, concat_axis=0, tiled=True)  21.2 us
    another operation x12, other arithmetic, orthonormal(): lax.linalg.triangular_solve(lower_factor, image, left_side=False, lower=T...  18.5 us
    dot_general x1, matrix products, local(): lax.dot_general(unfolded, unfolded, (((0,), (0,)), ((), ())), precision=p...  17.8 us
  transfers between devices with their start and end apart: 2, of which 2 were waited for; matrix products, arithmetic and copies ran while one was open for 0% of the time, Pallas kernels for 0%

commit v1 on v0

v1 whole, which is shorter than its diff:
```python
import functools
import math

import jax
import jax.numpy as jnp
from jax import lax
from jax.experimental import pallas as pl
from jax.experimental.pallas import tpu as pltpu
from jax.sharding import PartitionSpec as P

ITERS = 3
LANES = 128
SUBLANES = 8
MESH = pl.DeviceIdType.MESH
F32 = jnp.float32
BF16 = jnp.bfloat16
VMEM_LIMIT = 48 * 2**20

NX_CHIPS = 4
NY_CHIPS = 4
NZ_CHIPS = 8
CORES = 2
PLANE = NX_CHIPS * NY_CHIPS


def split3(value):
    high = value.astype(BF16)
    rest = value - high.astype(F32)
    middle = rest.astype(BF16)
    low = (rest - middle.astype(F32)).astype(BF16)
    return high, middle, low


def contract(left, right, left_dim, right_dim, precision=None):
    return lax.dot_general(
        left,
        right,
        (((left_dim,), (right_dim,)), ((), ())),
        precision=precision,
        preferred_element_type=F32,
    )


def lane_spread(block, lane):
    picks = jnp.full((SUBLANES, LANES), lane, jnp.int32)
    return jnp.take_along_axis(block, picks, axis=1, mode="promise_in_bounds")


def row_spread(block, row):
    return jnp.broadcast_to(block[row : row + 1, :], block.shape)


def eliminate(rows, tile, lane0):
    groups = len(rows)
    tiles = len(rows[0])
    rows = [list(group) for group in rows]
    sublane = lax.broadcasted_iota(jnp.int32, (SUBLANES, LANES), 0)
    scales = []
    for p in range(groups):
        columns = [
            [
                lane_spread(rows[q][tile], lane0 + SUBLANES * p + j) if q >= p else None
                for q in range(groups)
            ]
            for j in range(SUBLANES)
        ]
        scale = jnp.zeros((SUBLANES, LANES), F32)
        for j in range(SUBLANES):
            pivot = row_spread(columns[j][p], j)
            scale = jnp.where(sublane == j, lax.rsqrt(pivot), scale)
            inverse = 1.0 / pivot
            below = [q for q in range(p, groups) if not (q == p and j == SUBLANES - 1)]
            factor = {}
            for q in below:
                factor[q] = columns[j][q] * inverse
                if q == p:
                    factor[q] = jnp.where(sublane > j, factor[q], 0.0)
            for later in range(j + 1, SUBLANES):
                entry = row_spread(columns[later][p], j)
                for q in below:
                    columns[later][q] = columns[later][q] - factor[q] * entry
            for t in range(tiles):
                pivot_row = row_spread(rows[p][t], j)
                for q in below:
                    rows[q][t] = rows[q][t] - factor[q] * pivot_row
        scales.append(scale)
    return [[rows[q][t] * scales[q] for t in range(tiles)] for q in range(groups)]


def to_blocks(matrix):
    rows, columns = matrix.shape
    return [
        [
            matrix[r : r + SUBLANES, c : c + LANES]
            for c in range(0, columns, LANES)
        ]
        for r in range(0, rows, SUBLANES)
    ]


def from_blocks(blocks):
    return jnp.concatenate([jnp.concatenate(group, axis=1) for group in blocks], axis=0)


HIGHEST = lax.Precision.HIGHEST


def orthonormal(image_t):
    rank = image_t.shape[0]
    for repeat in range(2):
        inner_gram = contract(image_t, image_t, 1, 1, HIGHEST)
        padded = jnp.concatenate(
            [inner_gram, jnp.zeros((rank, LANES - rank), F32)], axis=1
        )
        blocks = [
            [c[0]] + w for c, w in zip(to_blocks(padded), to_blocks(image_t))
        ]
        blocks = eliminate(blocks, 0, 0)
        image_t = from_blocks([group[1:] for group in blocks])
    return image_t


def position():
    gx = lax.axis_index("gx")
    gy = lax.axis_index("gy")
    return gx // CORES, gx % CORES, gy % NY_CHIPS, gy // NY_CHIPS


def device(x, core, y, z):
    return (x * CORES + core, z * NY_CHIPS + y)


def far_first(steps):
    def hops(step):
        return sum(min(d, n - d) for d, n in zip(step, (NX_CHIPS, NY_CHIPS)))

    return sorted(steps, key=hops, reverse=True)


PLANE_STEPS = far_first(
    [(i, j) for i in range(NX_CHIPS) for j in range(NY_CHIPS) if i or j]
)
Z_STEPS = sorted(range(1, NZ_CHIPS), key=lambda d: -min(d, NZ_CHIPS - d))


def remote(source, target, send_sem, recv_sem, where):
    return pltpu.make_async_remote_copy(
        src_ref=source,
        dst_ref=target,
        send_sem=send_sem,
        recv_sem=recv_sem,
        device_id=where,
        device_id_type=MESH,
    )


def all_reduce(partial, full, from_core, mine, plane_in, z_out, z_in, send, recv):
    x, core, y, z = position()
    half = partial.shape[0] // CORES
    strip = half // PLANE
    place = x * NY_CHIPS + y
    own_half = pl.multiple_of(core * half, half)
    other_half = pl.multiple_of((1 - core) * half, half)
    other_core = device(x, 1 - core, y, z)

    swap = remote(
        partial.at[pl.ds(other_half, half)], from_core, send.at[0], recv.at[0], other_core
    )
    swap.start()
    swap.wait()
    summed = partial[pl.ds(own_half, half), :] + from_core[...]
    mine[...] = summed.reshape(mine.shape)

    for i, j in PLANE_STEPS:
        to_x, to_y = (x + i) % NX_CHIPS, (y + j) % NY_CHIPS
        remote(
            mine.at[to_x * NY_CHIPS + to_y],
            plane_in.at[place],
            send.at[1],
            recv.at[1],
            device(to_x, core, to_y, z),
        ).start()
    plane_in[place] = mine[place]
    others = pl.ds(0, PLANE - 1)
    landed = remote(mine.at[others], plane_in.at[others], send.at[1], recv.at[1], other_core)
    landed.wait()
    total = plane_in[0]
    for k in range(1, PLANE):
        total = total + plane_in[k]

    z_out[...] = total
    z_in[z] = total
    for d in Z_STEPS:
        to_z = (z + d) % NZ_CHIPS
        remote(
            z_out, z_in.at[z], send.at[2], recv.at[2], device(x, core, y, to_z)
        ).start()
    others = pl.ds(0, NZ_CHIPS - 1)
    landed = remote(z_in.at[others], z_in.at[others], send.at[2], recv.at[2], other_core)
    landed.wait()
    total = z_in[0]
    for k in range(1, NZ_CHIPS):
        total = total + z_in[k]

    own_strip = pl.ds(pl.multiple_of(own_half + place * strip, strip), strip)
    full[own_strip, :] = total
    for i, j in PLANE_STEPS:
        to_x, to_y = (x + i) % NX_CHIPS, (y + j) % NY_CHIPS
        remote(
            full.at[own_strip],
            full.at[own_strip],
            send.at[3],
            recv.at[3],
            device(to_x, core, to_y, z),
        ).start()
    others = pl.ds(0, (PLANE - 1) * strip)
    landed = remote(full.at[others], full.at[others], send.at[3], recv.at[3], other_core)
    landed.wait()

    rows = pl.ds(own_half, half)
    swap = remote(full.at[rows], full.at[rows], send.at[4], recv.at[4], other_core)
    swap.start()
    swap.wait()


def main_kernel(
    field,
    basis,
    core_out,
    zt_out,
    gram_x_out,
    staged,
    acc_same,
    acc_cross,
    partial,
    gram_z,
    gram_x,
    weights,
    core_parts,
    regrouped,
    *scratch,
):
    reduce_z, reduce_x = scratch[0:5], scratch[5:10]
    send_z, recv_z, send_x, recv_x, load_sem, core_sem, cell_send, cell_recv = scratch[10:]
    x, core, y, z = position()
    gx = x * CORES + core
    species = staged.shape[0]
    x_cells, y_cells, nz = staged.shape[1:]
    cells = x_cells * y_cells
    rank = basis.shape[1]
    groups = species * rank // LANES
    per_group = species // groups

    for s in range(species):
        pltpu.make_async_copy(field.at[:, :, s, :], staged.at[s], load_sem.at[s]).start()

    barrier = pltpu.get_barrier_semaphore()
    partners = [device(x, 1 - core, y, z)]
    for i, j in PLANE_STEPS:
        partners.append(device((x + i) % NX_CHIPS, core, (y + j) % NY_CHIPS, z))
    for d in Z_STEPS:
        partners.append(device(x, core, y, (z + d) % NZ_CHIPS))
    for i in range(1, NX_CHIPS):
        partners.append(device((x + i) % NX_CHIPS, 1 - core, y, z))
    for partner in partners:
        pl.semaphore_signal(barrier, inc=1, device_id=partner, device_id_type=MESH)

    acc_same[...] = jnp.zeros_like(acc_same)
    acc_cross[...] = jnp.zeros_like(acc_cross)

    def gram_step(s, carry):
        pltpu.make_async_copy(field.at[:, :, 0, :], staged.at[0], load_sem.at[s]).wait()
        high, middle, low = split3(staged[s].reshape(cells, nz))
        acc_same[...] += contract(high, high, 0, 0) + contract(middle, middle, 0, 0)
        acc_cross[...] += contract(high, middle, 0, 0) + contract(high, low, 0, 0)
        return carry

    lax.fori_loop(0, species, gram_step, 0)
    cross = acc_cross[...]
    partial[...] = acc_same[...] + (cross + cross.T)

    pl.semaphore_wait(barrier, len(partners))
    all_reduce(partial, gram_z, *reduce_z, send_z, recv_z)

    basis_t = basis[...].T
    for iteration in range(ITERS):
        basis_t = orthonormal(contract(basis_t, gram_z[...], 1, 0, HIGHEST))
    zt_out[...] = basis_t

    z_high, z_middle, _ = split3(basis_t)
    weights[...] = jnp.zeros_like(weights)
    for k in range(per_group):
        weights[k, k * rank : (k + 1) * rank, :] = z_high
        weights[k, LANES + k * rank : LANES + (k + 1) * rank, :] = z_middle

    half_y = y_cells // CORES
    for step in (2, 1, 3, 0):
        g = (x + step) % NX_CHIPS
        chunk = 4

        def core_step(i, carry):
            rows = pl.ds(i * chunk, chunk)
            total = jnp.zeros((chunk * y_cells, 2 * LANES), F32)
            for k in range(per_group):
                part = staged[g * per_group + k, rows].reshape(chunk * y_cells, nz)
                high = part.astype(BF16)
                middle = (part - high.astype(F32)).astype(BF16)
                total += contract(high, weights[k], 1, 1) + contract(middle, weights[k], 1, 1)
            core_parts[g, rows] = (total[:, :LANES] + total[:, LANES:]).reshape(
                chunk, y_cells, LANES
            )
            return carry

        lax.fori_loop(0, x_cells // chunk, core_step, 0)
        pltpu.make_async_copy(
            core_parts.at[g],
            core_out.at[:, :, pl.ds(pl.multiple_of(g * LANES, LANES), LANES)],
            core_sem.at[step],
        ).start()
        if step:
            for h in range(CORES):
                remote(
                    core_parts.at[g, :, pl.ds(h * half_y, half_y), :],
                    regrouped.at[gx],
                    cell_send,
                    cell_recv,
                    device(g, h, y, z),
                ).start()
        else:
            there = pl.multiple_of((1 - core) * half_y, half_y)
            remote(
                core_parts.at[g, :, pl.ds(there, half_y), :],
                regrouped.at[gx],
                cell_send,
                cell_recv,
                device(x, 1 - core, y, z),
            ).start()
            here = pl.multiple_of(core * half_y, half_y)
            regrouped[gx] = core_parts[g, :, pl.ds(here, half_y), :]

    others = pl.ds(0, CORES * NX_CHIPS - 1)
    landed = remote(
        regrouped.at[others], regrouped.at[others], cell_send, cell_recv, partners[0]
    )
    landed.wait()

    total_rows = regrouped.shape[0] * x_cells
    table = regrouped.reshape(total_rows * half_y, LANES)
    same = jnp.zeros((total_rows, total_rows), F32)
    cross = jnp.zeros((total_rows, total_rows), F32)
    for pair in range(half_y // 2):
        both = jnp.concatenate(
            [table[pl.ds(2 * pair + i, total_rows, stride=half_y), :] for i in range(2)],
            axis=1,
        )
        high, middle, low = split3(both)
        same += contract(high, high, 1, 1) + contract(middle, middle, 1, 1)
        cross += contract(high, middle, 1, 1) + contract(high, low, 1, 1)
    partial[...] = same + (cross + cross.T)
    all_reduce(partial, gram_x, *reduce_x, send_x, recv_x)
    gram_x_out[...] = gram_x[...]
    for g in range(groups):
        pltpu.make_async_copy(
            core_parts.at[0], core_out.at[:, :, pl.ds(0, LANES)], core_sem.at[g]
        ).wait()


def finish_kernel(column_count, core_in, zt, gram_x, core_out, z_out, tri_out, upper, sem):
    copy = pltpu.make_async_copy(core_in, core_out, sem)
    copy.start()
    z_out[...] = zt[...].T
    size = gram_x.shape[0]
    block = 32
    scale = 1.0 / math.sqrt(column_count)
    for r in range(0, size, block):
        first = r // LANES * LANES
        here = gram_x[r : r + block, first:]
        if r:
            here = here - contract(
                upper[0:r, r : r + block], upper[0:r, first:], 0, 0, HIGHEST
            )
        done = from_blocks(eliminate(to_blocks(here), 0, r - first))
        row = lax.broadcasted_iota(jnp.int32, done.shape, 0) + r
        column = lax.broadcasted_iota(jnp.int32, done.shape, 1) + first
        done = jnp.where(column >= row, done, 0.0)
        upper[r : r + block, first:] = done
        tri_out[r : r + block, first:] = done * scale
        if first:
            tri_out[r : r + block, :first] = jnp.zeros((block, first), F32)
    copy.wait()


def local(state_field, start_basis):
    x_cells, y_cells, species, nz = state_field.shape
    rank = start_basis.shape[1]
    columns = species * rank
    x_total = x_cells * lax.axis_size("gx")
    groups = columns // LANES
    half_y = y_cells // CORES
    vmem = pl.BlockSpec(memory_space=pltpu.VMEM)
    anywhere = pl.BlockSpec(memory_space=pl.ANY)

    def reduce_buffers(size):
        half = size // CORES
        strip = half // PLANE
        return [
            pltpu.VMEM((half, size), F32),
            pltpu.VMEM((PLANE, strip, size), F32),
            pltpu.VMEM((PLANE, strip, size), F32),
            pltpu.VMEM((strip, size), F32),
            pltpu.VMEM((NZ_CHIPS, strip, size), F32),
        ]

    dma = pltpu.SemaphoreType.DMA
    core_tensor, zt, gram_x = pl.pallas_call(
        main_kernel,
        out_shape=(
            jax.ShapeDtypeStruct((x_cells, y_cells, columns), F32),
            jax.ShapeDtypeStruct((rank, nz), F32),
            jax.ShapeDtypeStruct((x_total, x_total), F32),
        ),
        in_specs=[anywhere, vmem],
        out_specs=(anywhere, vmem, vmem),
        scratch_shapes=[
            pltpu.VMEM((species, x_cells, y_cells, nz), F32),
            pltpu.VMEM((nz, nz), F32),
            pltpu.VMEM((nz, nz), F32),
            pltpu.VMEM((nz, nz), F32),
            pltpu.VMEM((nz, nz), F32),
            pltpu.VMEM((x_total, x_total), F32),
            pltpu.VMEM((species // groups, 2 * LANES, nz), BF16),
            pltpu.VMEM((groups, x_cells, y_cells, LANES), F32),
            pltpu.VMEM((CORES * NX_CHIPS, x_cells, half_y, LANES), F32),
            *reduce_buffers(nz),
            *reduce_buffers(x_total),
            dma((5,)),
            dma((5,)),
            dma((5,)),
            dma((5,)),
            dma((species,)),
            dma((groups,)),
            dma,
            dma,
        ],
        compiler_params=pltpu.CompilerParams(
            collective_id=0, has_side_effects=True, vmem_limit_bytes=VMEM_LIMIT
        ),
        name="basis_core_gram",
    )(state_field, start_basis)

    column_count = y_cells * lax.axis_size("gy") * columns
    return pl.pallas_call(
        functools.partial(finish_kernel, column_count),
        out_shape=(
            jax.ShapeDtypeStruct((x_cells, y_cells, columns), F32),
            jax.ShapeDtypeStruct((nz, rank), F32),
            jax.ShapeDtypeStruct((x_total, x_total), F32),
        ),
        in_specs=[anywhere, vmem, vmem],
        out_specs=(anywhere, vmem, vmem),
        scratch_shapes=[pltpu.VMEM((x_total, x_total), F32), dma],
        compiler_params=pltpu.CompilerParams(vmem_limit_bytes=VMEM_LIMIT),
        name="x_factor",
    )(core_tensor, zt, gram_x)


def solution(mesh):
    return jax.shard_map(
        local,
        mesh=mesh,
        in_specs=(P("gx", "gy", None, None), P()),
        out_specs=(P("gx", "gy", None), P(), P()),
        check_vma=False,
    )
```

time: 676 us -> 84.8 us (0.13)
  waiting for transfers between devices: 499 us -> 0 us
  Pallas kernels: 0 us -> 82.4 us
  other arithmetic: 78.3 us -> 0 us
  matrix products: 36.2 us -> 0 us
  local copies, waits for them, and re-layouts: 24.3 us -> 1.55 us
  blocking collectives: 21.2 us -> 0 us
  between operations: 15.7 us -> 0.65 us
    psum x2 -> x0, waiting for transfers between devices: 499 us -> none  [the longest x1 253 us: local(): gram_z = lax.psum(local_gram, ('gx', 'gy'))]
    pallas_call x0 -> x2, Pallas kernels: none -> 82.4 us  [the longest x1 74.1 us: local(): pl.pallas_call(main_kernel, out_shape=(jax.ShapeDtypeStruct((x_cells, y_c...]
    another operation x36 -> x0, other arithmetic: 74.1 us -> none  [the longest x6 34 us: local(): jnp.linalg.cholesky(gram_x).T / jnp.sqrt(jnp.float32(column_count))]
    dot_general x12 -> x0, matrix products: 34.2 us -> none  [the longest x1 17.8 us: local(): lax.dot_general(unfolded, unfolded, (((0,), (0,)), ((), ())), precision=p...]
    all_to_all x1 -> x0, blocking collectives: 21.2 us -> none  [local(): lax.all_to_all(core_tensor, 'gx', split_axis=2, concat_axis=0, tiled=True)]
    reshape x3 -> x0, local copies, waits for them, and re-layouts: 7.96 us -> none  [the longest x2 7.38 us: local(): core_tensor = core_rows.reshape(x_cells, y_cells, species * rank_kept)]
    unnamed x9 -> x1, local copies, waits for them, and re-layouts: 8.08 us -> 0.85 us
  transfers between devices with their start and end apart: 2 -> 0, of which waited for: 2 -> 0; matrix products, arithmetic and copies ran while one was open for 0% -> 0% of each run, Pallas kernels for 0% -> 0%
where the time goes in v1:
time: 84.8 us; the launch traced here: 84.6 us
  Pallas kernels  82.4 us (97%)
  local copies, waits for them, and re-layouts  1.55 us (2%)
    pallas_call x1, Pallas kernels, local(): pl.pallas_call(main_kernel, out_shape=(jax.ShapeDtypeStruct((x_cells, y_c...  74.1 us
    pallas_call x1, Pallas kernels, local(): pl.pallas_call(functools.partial(finish_kernel, column_count), out_shape=...  8.31 us

profile of v1, /device:TPU:1, one launch (start us, length us, event | category | flops | bytes accessed | tf_op | source)
XLA Modules:
  0.0 84.6 jit_solution(1664478448991631938)
XLA Ops:
  0.6 0.9 %copy.5.basis = f32[256,32]{1,0:T(8,128)S(1)} copy(f32[256,32]{0,1:T(8,128)} %param.3) | data formatting | bytes 65536 | tf_op args[1]
  1.5 74.1 %basis_core_gram.1 = (f32[32,16,512]{2,1,0:T(8,128)S(1)}, f32[32,256]{1,0:T(8,128)S(1)}, f32[256,256]{1,0:T(8,128)S(1)}) custom-call(f32[32,16,16,256]{3,2,1,0:T(8,128)} %field.1, f32[256,32]{1,0:T(8,128)S(1)} %copy.5.basis), custom_call_target="tpu_custom_call" | custom-call | tf_op jit(solution)/shard_map/basis_core_gram/pallas_call | solution.py:415
  75.6 8.3 %x_factor.1 = (f32[32,16,512]{2,1,0:T(8,128)}, f32[256,32]{1,0:T(8,128)S(1)}, f32[256,256]{1,0:T(8,128)}) custom-call(f32[32,16,512]{2,1,0:T(8,128)S(1)} %get-tuple-element.6.core_in, f32[32,256]{1,0:T(8,128)S(1)} %get-tuple-element.7.zt, f32[256,256]{1,0:T(8,128)S(1)} %get-tuple-element.8.gram_x), custom_call_target="tpu_custom_call" | custom-call | tf_op jit(solution)/shard_map/x_factor/pallas_call | solution.py:452
  83.9 0.7 copy.6

commit v2 on v1

--- a/solution.py
+++ b/solution.py
@@ -29,6 +29,11 @@
     middle = rest.astype(BF16)
     low = (rest - middle.astype(F32)).astype(BF16)
     return high, middle, low
+
+
+def split2(value):
+    high = value.astype(BF16)
+    return high, (value - high.astype(F32)).astype(BF16)
 
 
 def contract(left, right, left_dim, right_dim, precision=None):
@@ -55,36 +60,35 @@
     tiles = len(rows[0])
     rows = [list(group) for group in rows]
     sublane = lax.broadcasted_iota(jnp.int32, (SUBLANES, LANES), 0)
-    scales = []
+    steps = range(SUBLANES)
     for p in range(groups):
+        below = range(p + 1, groups)
         columns = [
-            [
-                lane_spread(rows[q][tile], lane0 + SUBLANES * p + j) if q >= p else None
-                for q in range(groups)
-            ]
-            for j in range(SUBLANES)
+            {q: lane_spread(rows[q][tile], lane0 + SUBLANES * p + j) for q in range(p, groups)}
+            for j in steps
         ]
-        scale = jnp.zeros((SUBLANES, LANES), F32)
-        for j in range(SUBLANES):
-            pivot = row_spread(columns[j][p], j)
-            scale = jnp.where(sublane == j, lax.rsqrt(pivot), scale)
-            inverse = 1.0 / pivot
-            below = [q for q in range(p, groups) if not (q == p and j == SUBLANES - 1)]
-            factor = {}
+        corner = {(j, l): row_spread(columns[l][p], j) for j in steps for l in range(j, SUBLANES)}
+        lines = [[row_spread(rows[p][t], j) for j in steps] for t in range(tiles)]
+        done = list(rows[p])
+        for j in steps:
+            inverse = 1.0 / corner[j, j]
+            scale = lax.rsqrt(corner[j, j])
+            for l in range(j + 1, SUBLANES):
+                share = corner[j, l] * inverse
+                for n in range(l, SUBLANES):
+                    corner[l, n] = corner[l, n] - share * corner[j, n]
+                for t in range(tiles):
+                    lines[t][l] = lines[t][l] - share * lines[t][j]
             for q in below:
-                factor[q] = columns[j][q] * inverse
-                if q == p:
-                    factor[q] = jnp.where(sublane > j, factor[q], 0.0)
-            for later in range(j + 1, SUBLANES):
-                entry = row_spread(columns[later][p], j)
-                for q in below:
-                    columns[later][q] = columns[later][q] - factor[q] * entry
+                factor = columns[j][q] * inverse
+                for later in range(j + 1, SUBLANES):
+                    columns[later][q] = columns[later][q] - factor * corner[j, later]
+                for t in range(tiles):
+                    rows[q][t] = rows[q][t] - factor * lines[t][j]
             for t in range(tiles):
-                pivot_row = row_spread(rows[p][t], j)
-                for q in below:
-                    rows[q][t] = rows[q][t] - factor[q] * pivot_row
-        scales.append(scale)
-    return [[rows[q][t] * scales[q] for t in range(tiles)] for q in range(groups)]
+                done[t] = jnp.where(sublane == j, lines[t][j] * scale, done[t])
+        rows[p] = done
+    return rows
 
 
 def to_blocks(matrix):
@@ -107,7 +111,7 @@
 
 def orthonormal(image_t):
     rank = image_t.shape[0]
-    for repeat in range(2):
+    def one(r, image_t):
         inner_gram = contract(image_t, image_t, 1, 1, HIGHEST)
         padded = jnp.concatenate(
             [inner_gram, jnp.zeros((rank, LANES - rank), F32)], axis=1
@@ -116,8 +120,8 @@
             [c[0]] + w for c, w in zip(to_blocks(padded), to_blocks(image_t))
         ]
         blocks = eliminate(blocks, 0, 0)
-        image_t = from_blocks([group[1:] for group in blocks])
-    return image_t
+        return from_blocks([group[1:] for group in blocks])
+    return lax.fori_loop(0, 2, one, image_t)
 
 
 def position():
@@ -247,7 +251,7 @@
     species = staged.shape[0]
     x_cells, y_cells, nz = staged.shape[1:]
     cells = x_cells * y_cells
-    rank = basis.shape[1]
+    rank = basis.shape[0]
     groups = species * rank // LANES
     per_group = species // groups
 
@@ -268,26 +272,31 @@
     acc_same[...] = jnp.zeros_like(acc_same)
     acc_cross[...] = jnp.zeros_like(acc_cross)
 
-    def gram_step(s, carry):
-        pltpu.make_async_copy(field.at[:, :, 0, :], staged.at[0], load_sem.at[s]).wait()
-        high, middle, low = split3(staged[s].reshape(cells, nz))
+    batch = 4
+
+    def gram_step(i, carry):
+        for s in range(batch):
+            pltpu.make_async_copy(
+                field.at[:, :, 0, :], staged.at[0], load_sem.at[i * batch + s]
+            ).wait()
+        slab = staged[pl.ds(i * batch, batch)].reshape(batch * cells, nz)
+        high, middle = split2(slab)
         acc_same[...] += contract(high, high, 0, 0) + contract(middle, middle, 0, 0)
-        acc_cross[...] += contract(high, middle, 0, 0) + contract(high, low, 0, 0)
+        acc_cross[...] += contract(high, middle, 0, 0)
         return carry
 
-    lax.fori_loop(0, species, gram_step, 0)
+    lax.fori_loop(0, species // batch, gram_step, 0)
     cross = acc_cross[...]
     partial[...] = acc_same[...] + (cross + cross.T)
 
     pl.semaphore_wait(barrier, len(partners))
     all_reduce(partial, gram_z, *reduce_z, send_z, recv_z)
 
-    basis_t = basis[...].T
-    for iteration in range(ITERS):
-        basis_t = orthonormal(contract(basis_t, gram_z[...], 1, 0, HIGHEST))
+    basis_t = basis[...]
+    basis_t = lax.fori_loop(0, ITERS, lambda i, w: orthonormal(contract(w, gram_z[...], 1, 0, HIGHEST)), basis_t)
     zt_out[...] = basis_t
 
-    z_high, z_middle, _ = split3(basis_t)
+    z_high, z_middle = split2(basis_t)
     weights[...] = jnp.zeros_like(weights)
     for k in range(per_group):
         weights[k, k * rank : (k + 1) * rank, :] = z_high
@@ -296,22 +305,14 @@
     half_y = y_cells // CORES
     for step in (2, 1, 3, 0):
         g = (x + step) % NX_CHIPS
-        chunk = 4
-
-        def core_step(i, carry):
-            rows = pl.ds(i * chunk, chunk)
-            total = jnp.zeros((chunk * y_cells, 2 * LANES), F32)
-            for k in range(per_group):
-                part = staged[g * per_group + k, rows].reshape(chunk * y_cells, nz)
-                high = part.astype(BF16)
-                middle = (part - high.astype(F32)).astype(BF16)
-                total += contract(high, weights[k], 1, 1) + contract(middle, weights[k], 1, 1)
-            core_parts[g, rows] = (total[:, :LANES] + total[:, LANES:]).reshape(
-                chunk, y_cells, LANES
-            )
-            return carry
-
-        lax.fori_loop(0, x_cells // chunk, core_step, 0)
+        total = jnp.zeros((cells, 2 * LANES), F32)
+        for k in range(per_group):
+            part = staged[g * per_group + k].reshape(cells, nz)
+            high, middle = split2(part)
+            total += contract(high, weights[k], 1, 1) + contract(middle, weights[k], 1, 1)
+        core_parts[g] = (total[:, :LANES] + total[:, LANES:]).reshape(
+            x_cells, y_cells, LANES
+        )
         pltpu.make_async_copy(
             core_parts.at[g],
             core_out.at[:, :, pl.ds(pl.multiple_of(g * LANES, LANES), LANES)],
@@ -368,9 +369,9 @@
 def finish_kernel(column_count, core_in, zt, gram_x, core_out, z_out, tri_out, upper, sem):
     copy = pltpu.make_async_copy(core_in, core_out, sem)
     copy.start()
-    z_out[...] = zt[...].T
+    z_out[...] = zt[...]
     size = gram_x.shape[0]
-    block = 32
+    block = 64
     scale = 1.0 / math.sqrt(column_count)
     for r in range(0, size, block):
         first = r // LANES * LANES
@@ -446,14 +447,14 @@
             collective_id=0, has_side_effects=True, vmem_limit_bytes=VMEM_LIMIT
         ),
         name="basis_core_gram",
-    )(state_field, start_basis)
+    )(state_field, start_basis.T)
 
     column_count = y_cells * lax.axis_size("gy") * columns
-    return pl.pallas_call(
+    core_tensor, zt, x_triangle = pl.pallas_call(
         functools.partial(finish_kernel, column_count),
         out_shape=(
             jax.ShapeDtypeStruct((x_cells, y_cells, columns), F32),
-            jax.ShapeDtypeStruct((nz, rank), F32),
+            jax.ShapeDtypeStruct((rank, nz), F32),
             jax.ShapeDtypeStruct((x_total, x_total), F32),
         ),
         in_specs=[anywhere, vmem, vmem],
@@ -462,6 +463,7 @@
         compiler_params=pltpu.CompilerParams(vmem_limit_bytes=VMEM_LIMIT),
         name="x_factor",
     )(core_tensor, zt, gram_x)
+    return core_tensor, zt.T, x_triangle
 
 
 def solution(mesh):

time: 84.8 us -> 76 us (0.90)
  Pallas kernels: 82.4 us -> 74.5 us
    pallas_call x1, Pallas kernels: 74.1 us -> 67.2 us  [local(): pl.pallas_call(main_kernel, out_shape=(jax.ShapeDtypeStruct((x_cells, y_c...]
    pallas_call x1, Pallas kernels: 8.31 us -> 7.27 us  [local(): pl.pallas_call(functools.partial(finish_kernel, column_count), out_shape=...]
where the time goes in v2:
time: 76 us; the launch traced here: 75.9 us
  Pallas kernels  74.5 us (98%)
    pallas_call x1, Pallas kernels, local(): pl.pallas_call(main_kernel, out_shape=(jax.ShapeDtypeStruct((x_cells, y_c...  67.2 us
    pallas_call x1, Pallas kernels, local(): pl.pallas_call(functools.partial(finish_kernel, column_count), out_shape=...  7.27 us

profile of v2, /device:TPU:1, one launch (start us, length us, event | category | flops | bytes accessed | tf_op | source)
XLA Modules:
  0.0 75.9 jit_solution(3764436441065916041)
XLA Ops:
  0.6 0.0 copy-start
  0.6 0.7 copy-done
  1.4 67.2 %basis_core_gram.1 = (f32[32,16,512]{2,1,0:T(8,128)S(1)}, f32[32,256]{1,0:T(8,128)S(1)}, f32[256,256]{1,0:T(8,128)S(1)}) custom-call(f32[32,16,16,256]{3,2,1,0:T(8,128)} %field.1, f32[32,256]{1,0:T(8,128)S(1)} %bitcast.2), custom_call_target="tpu_custom_call" | custom-call | tf_op jit(solution)/shard_map/basis_core_gram/pallas_call | solution.py:416
  68.6 7.3 %x_factor.1 = (f32[32,16,512]{2,1,0:T(8,128)}, f32[32,256]{1,0:T(8,128)}, f32[256,256]{1,0:T(8,128)}) custom-call(f32[32,16,512]{2,1,0:T(8,128)S(1)} %get-tuple-element.9.core_in, f32[32,256]{1,0:T(8,128)S(1)} %get-tuple-element.10.zt, f32[256,256]{1,0:T(8,128)S(1)} %get-tuple-element.11.gram_x), custom_call_target="tpu_custom_call" | custom-call | tf_op jit(solution)/shard_map/x_factor/pallas_call | solution.py:453
Async XLA Ops:
  0.6 0.8 copy-start

commit v3 on v2

--- a/solution.py
+++ b/solution.py
@@ -109,19 +109,16 @@
 HIGHEST = lax.Precision.HIGHEST
 
 
-def orthonormal(image_t):
-    rank = image_t.shape[0]
-    def one(r, image_t):
-        inner_gram = contract(image_t, image_t, 1, 1, HIGHEST)
-        padded = jnp.concatenate(
-            [inner_gram, jnp.zeros((rank, LANES - rank), F32)], axis=1
-        )
-        blocks = [
-            [c[0]] + w for c, w in zip(to_blocks(padded), to_blocks(image_t))
-        ]
-        blocks = eliminate(blocks, 0, 0)
-        return from_blocks([group[1:] for group in blocks])
-    return lax.fori_loop(0, 2, one, image_t)
+def normalise(measured, image, transform):
+    rank = measured.shape[0]
+    inner_gram = contract(measured, measured, 1, 1, HIGHEST)
+    padded = jnp.concatenate(
+        [inner_gram, transform, jnp.zeros((rank, LANES - 2 * rank), F32)], axis=1
+    )
+    blocks = [[c[0]] + w for c, w in zip(to_blocks(padded), to_blocks(image))]
+    blocks = eliminate(blocks, 0, 0)
+    image = from_blocks([group[1:] for group in blocks])
+    return image, from_blocks([group[:1] for group in blocks])[:, rank : 2 * rank]
 
 
 def position():
@@ -240,12 +237,18 @@
     gram_z,
     gram_x,
     weights,
+    weights_low,
+    image_parts,
     core_parts,
     regrouped,
+    normalised,
+    basis_in,
     *scratch,
 ):
     reduce_z, reduce_x = scratch[0:5], scratch[5:10]
-    send_z, recv_z, send_x, recv_x, load_sem, core_sem, cell_send, cell_recv = scratch[10:]
+    send_z, recv_z, send_x, recv_x, load_sem, basis_sem, core_sem, cell_send, cell_recv = (
+        scratch[10:]
+    )
     x, core, y, z = position()
     gx = x * CORES + core
     species = staged.shape[0]
@@ -257,6 +260,8 @@
 
     for s in range(species):
         pltpu.make_async_copy(field.at[:, :, s, :], staged.at[s], load_sem.at[s]).start()
+
+    pltpu.make_async_copy(basis, basis_in, basis_sem).start()
 
     barrier = pltpu.get_barrier_semaphore()
     partners = [device(x, 1 - core, y, z)]
@@ -292,61 +297,119 @@
     pl.semaphore_wait(barrier, len(partners))
     all_reduce(partial, gram_z, *reduce_z, send_z, recv_z)
 
-    basis_t = basis[...]
-    basis_t = lax.fori_loop(0, ITERS, lambda i, w: orthonormal(contract(w, gram_z[...], 1, 0, HIGHEST)), basis_t)
+    pltpu.make_async_copy(basis, basis_in, basis_sem).wait()
+    identity = (
+        lax.broadcasted_iota(jnp.int32, (rank, rank), 0)
+        == lax.broadcasted_iota(jnp.int32, (rank, rank), 1)
+    ).astype(F32)
+
+    def orth_pass(i, image):
+        return normalise(image, image, identity)[0]
+
+    vectors = contract(basis_in[...], gram_z[...], 1, 0, HIGHEST)
+    vectors = lax.fori_loop(0, 2, orth_pass, vectors)
+    for iteration in range(1, ITERS - 1):
+        vectors = contract(vectors, gram_z[...], 1, 0, HIGHEST)
+        vectors = normalise(vectors, vectors, identity)[0]
+        if iteration < ITERS - 2:
+            vectors = normalise(vectors, vectors, identity)[0]
+    image = contract(vectors, gram_z[...], 1, 0, HIGHEST)
+
+    b_high, b_middle, b_low = split3(image)
+    weights[...] = jnp.zeros_like(weights)
+    weights_low[...] = jnp.zeros_like(weights_low)
+    for k in range(per_group):
+        own = slice(k * rank, (k + 1) * rank)
+        weights[k, own, :] = b_high
+        weights[k, LANES + k * rank : LANES + (k + 1) * rank, :] = b_middle
+        weights_low[k, own, :] = b_low
+
+    half_y = y_cells // CORES
+    parity = x % 2
+    for order in range(groups):
+        far = order < groups // 2
+        to_core = order % CORES if far else (1 - core if order == groups // 2 else core)
+        g = ((1 - parity) if far else parity) * CORES + to_core
+        total = jnp.zeros((cells, 2 * LANES), F32)
+        rest = jnp.zeros((cells, LANES), F32)
+        for k in range(per_group):
+            high, middle, low = split3(staged[g * per_group + k].reshape(cells, nz))
+            total += contract(high, weights[k], 1, 1) + contract(middle, weights[k], 1, 1)
+            rest += contract(low, weights[k, :LANES], 1, 1) + contract(high, weights_low[k], 1, 1)
+        image_parts[g] = (total[:, :LANES] + (total[:, LANES:] + rest)).reshape(
+            x_cells, y_cells, LANES
+        )
+        if far:
+            targets = [(x + 1) % NX_CHIPS, (x + 3) % NX_CHIPS]
+        elif order == groups // 2:
+            targets = [(x + 2) % NX_CHIPS, x]
+        else:
+            targets = [(x + 2) % NX_CHIPS]
+        for to_x in targets:
+            there = pl.multiple_of(to_x // 2 * half_y, half_y)
+            remote(
+                image_parts.at[g, :, pl.ds(there, half_y), :],
+                regrouped.at[gx],
+                cell_send,
+                cell_recv.at[gx],
+                device(to_x, to_core, y, z),
+            ).start()
+        if order == groups - 1:
+            here = pl.multiple_of(x // 2 * half_y, half_y)
+            regrouped[gx] = image_parts[g, :, pl.ds(here, half_y), :]
+
+    def last_pass(i, carry):
+        measured, image, transform = carry
+        image, transform = normalise(measured, image, transform)
+        return image, image, transform
+
+    _, basis_t, transform = lax.fori_loop(0, 3, last_pass, (vectors, image, identity))
     zt_out[...] = basis_t
 
     z_high, z_middle = split2(basis_t)
-    weights[...] = jnp.zeros_like(weights)
     for k in range(per_group):
         weights[k, k * rank : (k + 1) * rank, :] = z_high
         weights[k, LANES + k * rank : LANES + (k + 1) * rank, :] = z_middle
-
-    half_y = y_cells // CORES
-    for step in (2, 1, 3, 0):
-        g = (x + step) % NX_CHIPS
+    for g in range(groups):
         total = jnp.zeros((cells, 2 * LANES), F32)
         for k in range(per_group):
-            part = staged[g * per_group + k].reshape(cells, nz)
-            high, middle = split2(part)
+            high, middle = split2(staged[g * per_group + k].reshape(cells, nz))
             total += contract(high, weights[k], 1, 1) + contract(middle, weights[k], 1, 1)
         core_parts[g] = (total[:, :LANES] + total[:, LANES:]).reshape(
             x_cells, y_cells, LANES
         )
         pltpu.make_async_copy(
-            core_parts.at[g],
-            core_out.at[:, :, pl.ds(pl.multiple_of(g * LANES, LANES), LANES)],
-            core_sem.at[step],
+            core_parts.at[g], core_out.at[:, :, pl.ds(g * LANES, LANES)], core_sem.at[g]
         ).start()
-        if step:
-            for h in range(CORES):
-                remote(
-                    core_parts.at[g, :, pl.ds(h * half_y, half_y), :],
-                    regrouped.at[gx],
-                    cell_send,
-                    cell_recv,
-                    device(g, h, y, z),
-                ).start()
-        else:
-            there = pl.multiple_of((1 - core) * half_y, half_y)
+
+    wide = jnp.concatenate([transform] * per_group, axis=1)
+    wide = jnp.concatenate([wide] * per_group, axis=0)
+    row = lax.broadcasted_iota(jnp.int32, wide.shape, 0) // rank
+    lane = lax.broadcasted_iota(jnp.int32, wide.shape, 1) // rank
+    wide = jnp.where(row == lane, wide, 0.0)
+
+    chunk_rows = x_cells * half_y
+    for i, j in ((0, 0), (0, 1), (1, 0), (3, 0), (1, 1), (3, 1), (2, 1), (2, 0)):
+        source = (x + i) % NX_CHIPS * CORES + (core + j) % CORES
+        if i or j:
             remote(
-                core_parts.at[g, :, pl.ds(there, half_y), :],
-                regrouped.at[gx],
+                regrouped.at[source],
+                regrouped.at[source],
                 cell_send,
-                cell_recv,
-                device(x, 1 - core, y, z),
-            ).start()
-            here = pl.multiple_of(core * half_y, half_y)
-            regrouped[gx] = core_parts[g, :, pl.ds(here, half_y), :]
-
+                cell_recv.at[source],
+                partners[0],
+            ).wait_recv()
+        rows = pl.ds(pl.multiple_of(source * chunk_rows, chunk_rows), chunk_rows)
+        normalised[rows, :] = contract(
+            regrouped[source].reshape(chunk_rows, LANES), wide, 1, 1, HIGHEST
+        )
     others = pl.ds(0, CORES * NX_CHIPS - 1)
-    landed = remote(
-        regrouped.at[others], regrouped.at[others], cell_send, cell_recv, partners[0]
-    )
-    landed.wait()
+    remote(
+        regrouped.at[others], regrouped.at[others], cell_send, cell_recv.at[0], partners[0]
+    ).wait_send()
 
     total_rows = regrouped.shape[0] * x_cells
-    table = regrouped.reshape(total_rows * half_y, LANES)
+    table = normalised
     same = jnp.zeros((total_rows, total_rows), F32)
     cross = jnp.zeros((total_rows, total_rows), F32)
     for pair in range(half_y // 2):
@@ -420,7 +483,7 @@
             jax.ShapeDtypeStruct((rank, nz), F32),
             jax.ShapeDtypeStruct((x_total, x_total), F32),
         ),
-        in_specs=[anywhere, vmem],
+        in_specs=[anywhere, pl.BlockSpec(memory_space=pltpu.HBM)],
         out_specs=(anywhere, vmem, vmem),
         scratch_shapes=[
             pltpu.VMEM((species, x_cells, y_cells, nz), F32),
@@ -430,8 +493,12 @@
             pltpu.VMEM((nz, nz), F32),
             pltpu.VMEM((x_total, x_total), F32),
             pltpu.VMEM((species // groups, 2 * LANES, nz), BF16),
+            pltpu.VMEM((species // groups, LANES, nz), BF16),
+            pltpu.VMEM((groups, x_cells, y_cells, LANES), F32),
             pltpu.VMEM((groups, x_cells, y_cells, LANES), F32),
             pltpu.VMEM((CORES * NX_CHIPS, x_cells, half_y, LANES), F32),
+            pltpu.VMEM((x_total * half_y, LANES), F32),
+            pltpu.VMEM((rank, nz), F32),
             *reduce_buffers(nz),
             *reduce_buffers(x_total),
             dma((5,)),
@@ -439,9 +506,10 @@
             dma((5,)),
             dma((5,)),
             dma((species,)),
+            dma,
             dma((groups,)),
             dma,
-            dma,
+            dma((CORES * NX_CHIPS,)),
         ],
         compiler_params=pltpu.CompilerParams(
             collective_id=0, has_side_effects=True, vmem_limit_bytes=VMEM_LIMIT

time: 76 us -> 75 us (0.987)
  Pallas kernels: 74.5 us -> 73.3 us
    pallas_call x1, Pallas kernels: 67.2 us -> 66 us  [local(): pl.pallas_call(main_kernel, out_shape=(jax.ShapeDtypeStruct((x_cells, y_c...]
where the time goes in v3:
time: 75 us; the launch traced here: 74.8 us
  Pallas kernels  73.3 us (98%)
  between operations  0.81 us (1%)
  local copies, waits for them, and re-layouts  0.75 us (1%)
    pallas_call x1, Pallas kernels, local(): pl.pallas_call(main_kernel, out_shape=(jax.ShapeDtypeStruct((x_cells, y_c...  66 us
    pallas_call x1, Pallas kernels, local(): pl.pallas_call(functools.partial(finish_kernel, column_count), out_shape=...  7.27 us

profile of v3, /device:TPU:1, one launch (start us, length us, event | category | flops | bytes accessed | tf_op | source)
XLA Modules:
  0.0 74.8 jit_solution(8626390008259529492)
XLA Ops:
  0.6 0.0 copy-start
  0.6 0.7 %copy-done = f32[256,32]{0,1:T(8,128)S(1)} copy-done((f32[256,32]{0,1:T(8,128)S(1)}, f32[256,32]{0,1:T(8,128)}, u32[]{:S(2)}) %copy-start) | copy-done | bytes 32792
  1.4 66.0 %basis_core_gram.1 = (f32[32,16,512]{2,1,0:T(8,128)S(1)}, f32[32,256]{1,0:T(8,128)S(1)}, f32[256,256]{1,0:T(8,128)S(1)}) custom-call(f32[32,16,16,256]{3,2,1,0:T(8,128)} %field.1, f32[32,256]{1,0:T(8,128)S(1)} %bitcast.2), custom_call_target="tpu_custom_call" | custom-call | tf_op jit(solution)/shard_map/basis_core_gram/pallas_call | solution.py:479
  67.4 7.3 %x_factor.1 = (f32[32,16,512]{2,1,0:T(8,128)}, f32[32,256]{1,0:T(8,128)}, f32[256,256]{1,0:T(8,128)}) custom-call(f32[32,16,512]{2,1,0:T(8,128)S(1)} %get-tuple-element.9.core_in, f32[32,256]{1,0:T(8,128)S(1)} %get-tuple-element.10.zt, f32[256,256]{1,0:T(8,128)S(1)} %get-tuple-element.11.gram_x), custom_call_target="tpu_custom_call" | custom-call | tf_op jit(solution)/shard_map/x_factor/pallas_call | solution.py:521
Async XLA Ops:
  0.6 0.8 %copy-start = (f32[256,32]{0,1:T(8,128)S(1)}, f32[256,32]{0,1:T(8,128)}, u32[]{:S(2)}) copy-start(f32[256,32]{0,1:T(8,128)} %param.3) | copy-start | bytes 98308

commit v4 on v3

--- a/solution.py
+++ b/solution.py
@@ -274,6 +274,8 @@
     for partner in partners:
         pl.semaphore_signal(barrier, inc=1, device_id=partner, device_id_type=MESH)
 
+    weights[...] = jnp.zeros_like(weights)
+    weights_low[...] = jnp.zeros_like(weights_low)
     acc_same[...] = jnp.zeros_like(acc_same)
     acc_cross[...] = jnp.zeros_like(acc_cross)
 
@@ -316,8 +318,6 @@
     image = contract(vectors, gram_z[...], 1, 0, HIGHEST)
 
     b_high, b_middle, b_low = split3(image)
-    weights[...] = jnp.zeros_like(weights)
-    weights_low[...] = jnp.zeros_like(weights_low)
     for k in range(per_group):
         own = slice(k * rank, (k + 1) * rank)
         weights[k, own, :] = b_high

time: 75 us -> 75 us (level)
  no operation moved by 1% of the time
where the time goes in v4:
time: 75 us; the launch traced here: 74.8 us
  Pallas kernels  73.3 us (98%)
  between operations  0.81 us (1%)
  local copies, waits for them, and re-layouts  0.75 us (1%)
    pallas_call x1, Pallas kernels, local(): pl.pallas_call(main_kernel, out_shape=(jax.ShapeDtypeStruct((x_cells, y_c...  66 us
    pallas_call x1, Pallas kernels, local(): pl.pallas_call(functools.partial(finish_kernel, column_count), out_shape=...  7.27 us

profile of v4, /device:TPU:1, one launch (start us, length us, event | category | flops | bytes accessed | tf_op | source)
XLA Modules:
  0.0 74.8 jit_solution(4960587167133546321)
XLA Ops:
  0.6 0.0 copy-start
  0.6 0.7 %copy-done = f32[256,32]{0,1:T(8,128)S(1)} copy-done((f32[256,32]{0,1:T(8,128)S(1)}, f32[256,32]{0,1:T(8,128)}, u32[]{:S(2)}) %copy-start) | copy-done | bytes 32792
  1.4 66.0 %basis_core_gram.1 = (f32[32,16,512]{2,1,0:T(8,128)S(1)}, f32[32,256]{1,0:T(8,128)S(1)}, f32[256,256]{1,0:T(8,128)S(1)}) custom-call(f32[32,16,16,256]{3,2,1,0:T(8,128)} %field.1, f32[32,256]{1,0:T(8,128)S(1)} %bitcast.2), custom_call_target="tpu_custom_call" | custom-call | tf_op jit(solution)/shard_map/basis_core_gram/pallas_call | solution.py:479
  67.4 7.3 %x_factor.1 = (f32[32,16,512]{2,1,0:T(8,128)}, f32[32,256]{1,0:T(8,128)}, f32[256,256]{1,0:T(8,128)}) custom-call(f32[32,16,512]{2,1,0:T(8,128)S(1)} %get-tuple-element.9.core_in, f32[32,256]{1,0:T(8,128)S(1)} %get-tuple-element.10.zt, f32[256,256]{1,0:T(8,128)S(1)} %get-tuple-element.11.gram_x), custom_call_target="tpu_custom_call" | custom-call | tf_op jit(solution)/shard_map/x_factor/pallas_call | solution.py:521
Async XLA Ops:
  0.6 0.8 %copy-start = (f32[256,32]{0,1:T(8,128)S(1)}, f32[256,32]{0,1:T(8,128)}, u32[]{:S(2)}) copy-start(f32[256,32]{0,1:T(8,128)} %param.3) | copy-start | bytes 98308
